TPU v7x, 32 devices: a whole 2x2x4 slice. The times are simulated.
32 devices in a mesh: grp: 8 (over y, x, core), seq: 4 (over z).
Axes of the slice: x: 2, y: 2, z: 4, core: 2. Of those that a mesh axis runs over, the one named last changes fastest.
Arguments:
- inputs: bfloat16 [8, 2, 1536, 768], P('grp', None, 'seq'), may hold values from -6 to 6
- clip_frames: int32 [8, 2], P('grp'), may hold values from 96 to 384, as said below
- cotangent: bfloat16 [8, 2, 1536, 768], P('grp', None, 'seq'), may hold values from -6 to 6
- w_query: bfloat16 [768, 768], P(('grp', 'seq')), may hold values from -0.3125 to 0.3125
- w_key: bfloat16 [768, 768], P(('grp', 'seq')), may hold values from -0.3125 to 0.3125
- w_value: bfloat16 [768, 768], P(('grp', 'seq')), may hold values from -0.21875 to 0.21875
- w_out: bfloat16 [768, 768], P(('grp', 'seq')), may hold values from -0.875 to 0.875
- w_up: bfloat16 [768, 3072], P(('grp', 'seq')), may hold values from -0.21875 to 0.21875
- w_down: bfloat16 [3072, 768], P(('grp', 'seq')), may hold values from -0.15625 to 0.15625
- b_query: bfloat16 [768], P(('grp', 'seq')), may hold values from -3 to 3
- b_value: bfloat16 [768], P(('grp', 'seq')), may hold values from -1.796875 to 1.796875
- b_out: bfloat16 [768], P(('grp', 'seq')), may hold values from -3 to 3
- b_up: bfloat16 [3072], P(('grp', 'seq')), may hold values from -3 to 3
- b_down: bfloat16 [768], P(('grp', 'seq')), may hold values from -3 to 3
- gain_one: bfloat16 [768], P(('grp', 'seq')), may hold values from 0.5 to 1.5
- shift_one: bfloat16 [768], P(('grp', 'seq')), may hold values from -1.796875 to 1.796875
- gain_two: bfloat16 [768], P(('grp', 'seq')), may hold values from 0.5 to 1.5
- shift_two: bfloat16 [768], P(('grp', 'seq')), may hold values from -1.796875 to 1.796875
Outputs:
- layer_out: bfloat16 [8, 2, 1536, 768], P('grp', None, 'seq')
- grad_inputs: bfloat16 [8, 2, 1536, 768], P('grp', None, 'seq')
- grad_w_query: float32 [768, 768], P(('grp', 'seq'))
- grad_w_key: float32 [768, 768], P(('grp', 'seq'))
- grad_w_value: float32 [768, 768], P(('grp', 'seq'))
- grad_w_out: float32 [768, 768], P(('grp', 'seq'))
- grad_w_up: float32 [768, 3072], P(('grp', 'seq'))
- grad_w_down: float32 [3072, 768], P(('grp', 'seq'))
- grad_b_query: float32 [768], P(('grp', 'seq'))
- grad_b_value: float32 [768], P(('grp', 'seq'))
- grad_b_out: float32 [768], P(('grp', 'seq'))
- grad_b_up: float32 [3072], P(('grp', 'seq'))
- grad_b_down: float32 [768], P(('grp', 'seq'))
- grad_gain_one: float32 [768], P(('grp', 'seq'))
- grad_shift_one: float32 [768], P(('grp', 'seq'))
- grad_gain_two: float32 [768], P(('grp', 'seq'))
- grad_shift_two: float32 [768], P(('grp', 'seq'))
Inputs may be any that keep to these rules, and one draw needn't show every extreme that they name: Every slice of clip slot (g, s) holds clip_frames[g, s] live frames at its start; in every draw one slot has exactly 384 and another exactly 96.
All inputs are finite; a program needn't handle non-finite values.
Results may differ from a plain program's by a relative error of at most 0.015.
Values may be sent and summed in bfloat16 or wider, within the bound.
A program may use at most 192 MiB of HBM per device.

v0:
```python
import jax
import jax.numpy as jnp
from jax import lax
from jax.sharding import PartitionSpec as P

HEAD = 64
epsilon = 1e-05
score_scale = 0.125
sqrt_half = 0.7071067811865476
inv_root_tau = 0.3989422804014327


def standardize(token_rows):
    row_mean = jnp.mean(token_rows, -1, keepdims=True)
    centred = token_rows - row_mean
    inverse = lax.rsqrt(jnp.mean(centred * centred, -1, keepdims=True) + epsilon)
    return (centred * inverse, inverse)


def norm_back(grad_out, normed, inverse, gain_vec):
    scaled = grad_out * gain_vec
    grad_rows = inverse * (
        scaled
        - jnp.mean(scaled, -1, keepdims=True)
        - normed * jnp.mean(scaled * normed, -1, keepdims=True)
    )
    return (grad_rows, jnp.sum(grad_out * normed, 0), jnp.sum(grad_out, 0))


def gelu_slope(hidden):
    return (
        0.5 * (1.0 + lax.erf(hidden * sqrt_half))
        + hidden * jnp.exp(-0.5 * hidden * hidden) * inv_root_tau
    )


def split_heads(block, pair_count):
    slot_count, length, width = block.shape
    return block.reshape(slot_count, length, pair_count, 2, HEAD).transpose(2, 0, 1, 3, 4)


def merge_heads(block):
    pair_count, slot_count, length, twin_heads, head_size = block.shape
    return block.transpose(1, 2, 0, 3, 4).reshape(
        slot_count, length, pair_count * twin_heads * head_size
    )


def body(
    inputs,
    clip_frames,
    cotangent,
    w_query,
    w_key,
    w_value,
    w_out,
    w_up,
    w_down,
    b_query,
    b_value,
    b_out,
    b_up,
    b_down,
    gain_one,
    shift_one,
    gain_two,
    shift_two,
):
    shards = (
        w_query,
        w_key,
        w_value,
        w_out,
        w_up,
        w_down,
        b_query,
        b_value,
        b_out,
        b_up,
        b_down,
        gain_one,
        shift_one,
        gain_two,
        shift_two,
    )
    (
        wq_full,
        wk_full,
        wv_full,
        wo_full,
        up_full,
        down_full,
        bq_full,
        bv_full,
        bo_full,
        bu_full,
        bd_full,
        gain_first,
        shift_first,
        gain_second,
        shift_second,
    ) = (
        lax.all_gather(shards[0], ("grp", "seq"), axis=0, tiled=True),
        lax.all_gather(shards[1], ("grp", "seq"), axis=0, tiled=True),
        lax.all_gather(shards[2], ("grp", "seq"), axis=0, tiled=True),
        lax.all_gather(shards[3], ("grp", "seq"), axis=0, tiled=True),
        lax.all_gather(shards[4], ("grp", "seq"), axis=0, tiled=True),
        lax.all_gather(shards[5], ("grp", "seq"), axis=0, tiled=True),
        lax.all_gather(shards[6], ("grp", "seq"), axis=0, tiled=True),
        lax.all_gather(shards[7], ("grp", "seq"), axis=0, tiled=True),
        lax.all_gather(shards[8], ("grp", "seq"), axis=0, tiled=True),
        lax.all_gather(shards[9], ("grp", "seq"), axis=0, tiled=True),
        lax.all_gather(shards[10], ("grp", "seq"), axis=0, tiled=True),
        lax.all_gather(shards[11], ("grp", "seq"), axis=0, tiled=True),
        lax.all_gather(shards[12], ("grp", "seq"), axis=0, tiled=True),
        lax.all_gather(shards[13], ("grp", "seq"), axis=0, tiled=True),
        lax.all_gather(shards[14], ("grp", "seq"), axis=0, tiled=True),
    )
    slot_count, slice_len, width = (inputs.shape[1], inputs.shape[2], inputs.shape[3])
    row_count = slot_count * slice_len
    pair_count = width // (2 * HEAD)
    token_rows = inputs[0].astype(jnp.float32).reshape(row_count, width)
    normed_one, inverse_one = standardize(token_rows)
    first_in = (
        normed_one * gain_first.astype(jnp.float32) + shift_first.astype(jnp.float32)
    ).astype(jnp.bfloat16)
    queries = (
        jnp.dot(first_in, wq_full, preferred_element_type=jnp.float32) + bq_full.astype(jnp.float32)
    ).astype(jnp.bfloat16)
    key_local = jnp.dot(first_in, wk_full, preferred_element_type=jnp.float32).astype(jnp.bfloat16)
    value_local = (
        jnp.dot(first_in, wv_full, preferred_element_type=jnp.float32) + bv_full.astype(jnp.float32)
    ).astype(jnp.bfloat16)
    key_all, value_all = (
        lax.all_gather(key_local.reshape(slot_count, slice_len, width), "seq", axis=1, tiled=True),
        lax.all_gather(
            value_local.reshape(slot_count, slice_len, width), "seq", axis=1, tiled=True
        ),
    )
    clip_len = key_all.shape[1]
    offsets = jnp.arange(clip_len, dtype=jnp.int32) % slice_len
    live_keys = offsets[None, :] < clip_frames[0][:, None]
    query_heads = split_heads(queries.reshape(slot_count, slice_len, width), pair_count)
    key_heads = split_heads(key_all, pair_count)
    value_heads = split_heads(value_all, pair_count)

    def masked_scores(query_block, key_block, live_mask):
        scores = (
            jnp.einsum(
                "cqhd,ckhd->chqk", query_block, key_block, preferred_element_type=jnp.float32
            )
            * score_scale
        )
        return jnp.where(live_mask[:, None, None, :], scores, -1e30)

    def attend(pieces):
        query_block, key_block, value_block = pieces
        scores = masked_scores(query_block, key_block, live_keys)
        row_max = jnp.max(scores, -1, keepdims=True)
        exponent = jnp.exp(scores - row_max)
        row_sum = jnp.sum(exponent, -1, keepdims=True)
        weights = (exponent / row_sum).astype(jnp.bfloat16)
        mixed_block = jnp.einsum(
            "chqk,ckhd->cqhd", weights, value_block, preferred_element_type=jnp.float32
        )
        return (mixed_block, (row_max + jnp.log(row_sum))[..., 0])

    mixed_heads, logsum = lax.map(attend, (query_heads, key_heads, value_heads))
    mixed_low = merge_heads(mixed_heads).reshape(row_count, width).astype(jnp.bfloat16)
    branch = jnp.dot(mixed_low, wo_full, preferred_element_type=jnp.float32) + bo_full.astype(
        jnp.float32
    )
    middle = token_rows + branch
    normed_two, inverse_two = standardize(middle)
    second_in = (
        normed_two * gain_second.astype(jnp.float32) + shift_second.astype(jnp.float32)
    ).astype(jnp.bfloat16)
    hidden = jnp.dot(second_in, up_full, preferred_element_type=jnp.float32) + bu_full.astype(
        jnp.float32
    )
    active_low = jax.nn.gelu(hidden, approximate=False).astype(jnp.bfloat16)
    result = (
        middle
        + jnp.dot(active_low, down_full, preferred_element_type=jnp.float32)
        + bd_full.astype(jnp.float32)
    )
    layer_out = result.astype(jnp.bfloat16).reshape(inputs.shape)
    (
        wq_full,
        wk_full,
        wv_full,
        wo_full,
        up_full,
        down_full,
        bq_full,
        bv_full,
        bo_full,
        bu_full,
        bd_full,
        gain_first,
        shift_first,
        gain_second,
        shift_second,
    ) = (
        lax.all_gather(shards[0], ("grp", "seq"), axis=0, tiled=True),
        lax.all_gather(shards[1], ("grp", "seq"), axis=0, tiled=True),
        lax.all_gather(shards[2], ("grp", "seq"), axis=0, tiled=True),
        lax.all_gather(shards[3], ("grp", "seq"), axis=0, tiled=True),
        lax.all_gather(shards[4], ("grp", "seq"), axis=0, tiled=True),
        lax.all_gather(shards[5], ("grp", "seq"), axis=0, tiled=True),
        lax.all_gather(shards[6], ("grp", "seq"), axis=0, tiled=True),
        lax.all_gather(shards[7], ("grp", "seq"), axis=0, tiled=True),
        lax.all_gather(shards[8], ("grp", "seq"), axis=0, tiled=True),
        lax.all_gather(shards[9], ("grp", "seq"), axis=0, tiled=True),
        lax.all_gather(shards[10], ("grp", "seq"), axis=0, tiled=True),
        lax.all_gather(shards[11], ("grp", "seq"), axis=0, tiled=True),
        lax.all_gather(shards[12], ("grp", "seq"), axis=0, tiled=True),
        lax.all_gather(shards[13], ("grp", "seq"), axis=0, tiled=True),
        lax.all_gather(shards[14], ("grp", "seq"), axis=0, tiled=True),
    )
    grad_top = cotangent[0].reshape(row_count, width)
    grad_rows = grad_top.astype(jnp.float32)
    grad_down = jnp.dot(active_low.T, grad_top, preferred_element_type=jnp.float32)
    gbias_down = jnp.sum(grad_rows, 0)
    grad_active = jnp.dot(grad_top, down_full.T, preferred_element_type=jnp.float32)
    grad_hidden = (grad_active * gelu_slope(hidden)).astype(jnp.bfloat16)
    grad_up = jnp.dot(second_in.T, grad_hidden, preferred_element_type=jnp.float32)
    gbias_up = jnp.sum(grad_hidden.astype(jnp.float32), 0)
    grad_second = jnp.dot(grad_hidden, up_full.T, preferred_element_type=jnp.float32)
    grad_norm_two, grad_gain_two, grad_shift_two = norm_back(
        grad_second, normed_two, inverse_two, gain_second.astype(jnp.float32)
    )
    grad_middle = grad_rows + grad_norm_two
    grad_branch = grad_middle.astype(jnp.bfloat16)
    grad_out = jnp.dot(mixed_low.T, grad_branch, preferred_element_type=jnp.float32)
    gbias_out = jnp.sum(grad_branch.astype(jnp.float32), 0)
    grad_mixed = jnp.dot(grad_branch, wo_full.T, preferred_element_type=jnp.float32).astype(
        jnp.bfloat16
    )
    mixed_grad_heads = split_heads(grad_mixed.reshape(slot_count, slice_len, width), pair_count)

    def score_grads(query_block, key_block, value_block, grad_block, logsum_block, live_mask):
        scores = masked_scores(query_block, key_block, live_mask)
        weights = jnp.exp(scores - logsum_block[..., None])
        grad_weights = jnp.einsum(
            "cqhd,ckhd->chqk", grad_block, value_block, preferred_element_type=jnp.float32
        )
        return (weights, grad_weights)

    def attend_back(pieces):
        query_block, key_block, value_block, grad_block, logsum_block = pieces
        weights, grad_weights = score_grads(
            query_block, key_block, value_block, grad_block, logsum_block, live_keys
        )
        inner_sum = jnp.sum(weights * grad_weights, -1, keepdims=True)
        grad_scores = (weights * (grad_weights - inner_sum)).astype(jnp.bfloat16)
        grad_query_block = (
            jnp.einsum(
                "chqk,ckhd->cqhd", grad_scores, key_block, preferred_element_type=jnp.float32
            )
            * score_scale
        )
        grad_key_block = (
            jnp.einsum(
                "chqk,cqhd->ckhd", grad_scores, query_block, preferred_element_type=jnp.float32
            )
            * score_scale
        )
        grad_value_block = jnp.einsum(
            "chqk,cqhd->ckhd",
            weights.astype(jnp.bfloat16),
            grad_block,
            preferred_element_type=jnp.float32,
        )
        return (grad_query_block, grad_key_block, grad_value_block)

    gq_heads, gk_heads, gv_heads = lax.map(
        attend_back, (query_heads, key_heads, value_heads, mixed_grad_heads, logsum)
    )
    key_grads, value_grads = (
        lax.psum_scatter(
            merge_heads(gk_heads).astype(jnp.bfloat16), "seq", scatter_dimension=1, tiled=True
        ).astype(jnp.float32),
        lax.psum_scatter(
            merge_heads(gv_heads).astype(jnp.bfloat16), "seq", scatter_dimension=1, tiled=True
        ).astype(jnp.float32),
    )
    grad_key = key_grads.reshape(row_count, width).astype(jnp.bfloat16)
    grad_value = value_grads.reshape(row_count, width).astype(jnp.bfloat16)
    grad_query = merge_heads(gq_heads).reshape(row_count, width).astype(jnp.bfloat16)
    gw_query = jnp.dot(first_in.T, grad_query, preferred_element_type=jnp.float32)
    gw_key = jnp.dot(first_in.T, grad_key, preferred_element_type=jnp.float32)
    gw_value = jnp.dot(first_in.T, grad_value, preferred_element_type=jnp.float32)
    gbias_query = jnp.sum(grad_query.astype(jnp.float32), 0)
    gbias_value = jnp.sum(grad_value.astype(jnp.float32), 0)
    grad_first = jnp.dot(grad_query, wq_full.T, preferred_element_type=jnp.float32)
    grad_first = grad_first + jnp.dot(grad_key, wk_full.T, preferred_element_type=jnp.float32)
    grad_first = grad_first + jnp.dot(grad_value, wv_full.T, preferred_element_type=jnp.float32)
    grad_norm_one, grad_gain_one, grad_shift_one = norm_back(
        grad_first, normed_one, inverse_one, gain_first.astype(jnp.float32)
    )
    grad_inputs = (grad_middle + grad_norm_one).astype(jnp.bfloat16).reshape(inputs.shape)
    summed_all = (
        lax.psum_scatter(gw_query, ("grp", "seq"), scatter_dimension=0, tiled=True),
        lax.psum_scatter(gw_key, ("grp", "seq"), scatter_dimension=0, tiled=True),
        lax.psum_scatter(gw_value, ("grp", "seq"), scatter_dimension=0, tiled=True),
        lax.psum_scatter(grad_out, ("grp", "seq"), scatter_dimension=0, tiled=True),
        lax.psum_scatter(grad_up, ("grp", "seq"), scatter_dimension=0, tiled=True),
        lax.psum_scatter(grad_down, ("grp", "seq"), scatter_dimension=0, tiled=True),
        lax.psum_scatter(gbias_query, ("grp", "seq"), scatter_dimension=0, tiled=True),
        lax.psum_scatter(gbias_value, ("grp", "seq"), scatter_dimension=0, tiled=True),
        lax.psum_scatter(gbias_out, ("grp", "seq"), scatter_dimension=0, tiled=True),
        lax.psum_scatter(gbias_up, ("grp", "seq"), scatter_dimension=0, tiled=True),
        lax.psum_scatter(gbias_down, ("grp", "seq"), scatter_dimension=0, tiled=True),
        lax.psum_scatter(grad_gain_one, ("grp", "seq"), scatter_dimension=0, tiled=True),
        lax.psum_scatter(grad_shift_one, ("grp", "seq"), scatter_dimension=0, tiled=True),
        lax.psum_scatter(grad_gain_two, ("grp", "seq"), scatter_dimension=0, tiled=True),
        lax.psum_scatter(grad_shift_two, ("grp", "seq"), scatter_dimension=0, tiled=True),
    )
    return (
        layer_out,
        grad_inputs,
        summed_all[0],
        summed_all[1],
        summed_all[2],
        summed_all[3],
        summed_all[4],
        summed_all[5],
        summed_all[6],
        summed_all[7],
        summed_all[8],
        summed_all[9],
        summed_all[10],
        summed_all[11],
        summed_all[12],
        summed_all[13],
        summed_all[14],
    )


def solution(mesh):
    return jax.shard_map(
        body,
        mesh=mesh,
        in_specs=(
            P("grp", None, "seq", None),
            P("grp", None),
            P("grp", None, "seq", None),
            P(("grp", "seq"), None),
            P(("grp", "seq"), None),
            P(("grp", "seq"), None),
            P(("grp", "seq"), None),
            P(("grp", "seq"), None),
            P(("grp", "seq"), None),
            P(("grp", "seq")),
            P(("grp", "seq")),
            P(("grp", "seq")),
            P(("grp", "seq")),
            P(("grp", "seq")),
            P(("grp", "seq")),
            P(("grp", "seq")),
            P(("grp", "seq")),
            P(("grp", "seq")),
        ),
        out_specs=(
            P("grp", None, "seq", None),
            P("grp", None, "seq", None),
            P(("grp", "seq"), None),
            P(("grp", "seq"), None),
            P(("grp", "seq"), None),
            P(("grp", "seq"), None),
            P(("grp", "seq"), None),
            P(("grp", "seq"), None),
            P(("grp", "seq")),
            P(("grp", "seq")),
            P(("grp", "seq")),
            P(("grp", "seq")),
            P(("grp", "seq")),
            P(("grp", "seq")),
            P(("grp", "seq")),
            P(("grp", "seq")),
            P(("grp", "seq")),
        ),
        check_vma=False,
    )
```

profile of v0, /device:TPU:0, one launch (start us, length us, event | category | flops | bytes accessed | tf_op | source)
XLA Modules:
  0.0 1670.7 jit_solution(11885890830249403467)
XLA Ops:
  17.0 42.7 %all-reduce.19 = (bf16[768]{0:T(1024)(128)(2,1)S(1)}, bf16[768]{0:T(1024)(128)(2,1)S(1)}, bf16[768]{0:T(1024)(128)(2,1)S(1)}, bf16[768]{0:T(1024)(128)(2,1)}, bf...) all-reduce(bf16[768]{0:T(1024)(128)(2,1)S(1)} %dynamic-update-slice, ...), channel_id=1, replica_groups=mesh['grp'=8,'seq'=4] {'grp','seq'}, use_global_device_ids=true, to_apply=%add.1 | all-reduce | flops 9216 | bytes 36864
  64.1 3.9 all-gather.9.cloned.1.call-done
  71.9 51.8 %all-gather.15.cloned.1.call-done = bf16[768,768]{1,0:T(8,128)(2,1)} async-done(((bf16[24,768]{1,0:T(8,128)(2,1)}), bf16[768,768]{1,0:T(8,128)(2,1)}) %all-gather.15.cloned.1.call-update) | async-done | bytes 1179664 | tf_op jit(solution)/shard_map/all_gather | solution.py:104
  135.0 44.6 %all-gather.13.cloned.1.call-done = bf16[768,768]{1,0:T(8,128)(2,1)} async-done(((bf16[24,768]{1,0:T(8,128)(2,1)}), bf16[768,768]{1,0:T(8,128)(2,1)}) %all-gather.13.cloned.1.call-update) | async-done | bytes 1179664 | tf_op jit(solution)/shard_map/all_gather | solution.py:103
  183.1 86.8 %all-gather.11.cloned.1.call-done = bf16[2,1536,768]{1,2,0:T(8,128)(2,1)} async-done(((bf16[2,384,768]{1,2,0:T(8,128)(2,1)}), bf16[2,1536,768]{1,2,0:T(8,128)(2,1)}) %all-gather.11.cloned.1.call-update) | async-done | bytes 4718608 | tf_op jit(solution)/shard_map/all_gather | solution.py:136
  270.0 5.0 copy.72
  275.0 84.9 %all-gather.17.cloned.1.call-done = bf16[2,1536,768]{1,2,0:T(8,128)(2,1)} async-done(((bf16[2,384,768]{1,2,0:T(8,128)(2,1)}), bf16[2,1536,768]{1,2,0:T(8,128)(2,1)}) %all-gather.17.cloned.1.call-update) | async-done | bytes 4718608 | tf_op jit(solution)/shard_map/all_gather | solution.py:135
  359.9 5.0 copy.74
  365.0 54.2 %while.28 = (s32[]{:T(128)}, bf16[6,2,384,2,64]{2,4,3,1,0:T(8,128)(2,1)S(1)}, f32[6,2,2,384]{3,2,1,0:T(2,128)}, bf16[6,2,1536,2,64]{2,4,3,1,0:T(8,128)(2,1)}, bf...) while((s32[]{:T(128)}, ...), condition=%wide.region_5.6_spmd.clone, body=%wide.region_2.5_spmd.clone.sunk | while | flops 632292864 | bytes 30550128 | solution.py:168
  369.9 3.6 fusion.148
  378.9 3.6 fusion.148
  406.0 3.6 fusion.148
  415.1 3.5 fusion.148
  425.6 54.9 %all-gather.21.cloned.1.call-done = bf16[768,3072]{1,0:T(8,128)(2,1)} async-done(((bf16[24,3072]{1,0:T(8,128)(2,1)}), bf16[768,3072]{1,0:T(8,128)(2,1)}) %all-gather.21.cloned.1.call-update) | async-done | bytes 4718608 | tf_op jit(solution)/shard_map/all_gather | solution.py:107
  480.5 28.1 %fusion.49 = (bf16[768,3072]{1,0:T(8,128)(2,1)}, f32[768,3072]{1,0:T(8,128)}) fusion(f32[3072]{0:T(1024)} %convert_element_type.182, bf16[768,3072]{1,0:T(8,128)(2,1)} %all-gather.21.cloned.1.call-done, f32[768,768]{1,0:T(8,128)S(1)} %get-tuple-element.288, f32[768]{0:T(1024)} %convert_element_type.180, f32[768]{0:T(1024)S(1)} %convert_element_type.179, ...), kind=kOutput, calls=%fused_computation.59 | convolution fusion | flops 3782541312 | bytes 21258240 | tf_op jit(solution)/shard_map/dot_general | solution.py:178
  508.6 37.1 %all-gather.23.cloned.1.call-done = bf16[3072,768]{1,0:T(8,128)(2,1)} async-done(((bf16[96,768]{1,0:T(8,128)(2,1)}), bf16[3072,768]{1,0:T(8,128)(2,1)}) %all-gather.23.cloned.1.call-update) | async-done | bytes 4718608 | tf_op jit(solution)/shard_map/all_gather | solution.py:108
  545.7 10.2 convert_reduce_fusion
  555.9 4.9 multiply_reduce_fusion.1
  570.1 201.9 %while.29 = (s32[]{:T(128)}, bf16[6,2,384,2,64]{2,4,3,1,0:T(8,128)(2,1)}, bf16[6,2,1536,2,64]{2,4,3,0,1:T(8,128)(2,1)}, bf16[6,2,1536,2,64]{2,4,3,0,1:T(8,128)(2...) while((s32[]{:T(128)}, ...), condition=%wide.region_12.13_spmd.clone, body=%wide.region_10.12_spmd.clone.sunk | while | flops 1531676160 | bytes 153400592 | solution.py:277
  574.5 8.7 multiply_reduce_fusion.7
  583.2 9.4 multiply_convert_fusion.2
  592.6 4.9 fusion.156
  597.5 4.3 fusion.157
  608.2 8.7 multiply_reduce_fusion.7
  616.9 9.4 multiply_convert_fusion.2
  626.3 4.9 fusion.156
  631.2 4.3 fusion.157
  641.9 8.7 multiply_reduce_fusion.7
  650.5 9.4 multiply_convert_fusion.2
  659.9 4.9 fusion.156
  664.8 4.3 fusion.157
  675.5 8.7 multiply_reduce_fusion.7
  684.2 9.4 multiply_convert_fusion.2
  693.5 4.9 fusion.156
  698.5 4.3 fusion.157
  709.1 8.7 multiply_reduce_fusion.7
  717.8 9.4 multiply_convert_fusion.2
  727.1 4.9 fusion.156
  732.1 4.3 fusion.157
  742.7 8.7 multiply_reduce_fusion.7
  751.4 9.4 multiply_convert_fusion.2
  760.8 4.9 fusion.156
  765.7 4.3 fusion.157
  771.9 12.5 copy.86
  784.4 5.5 copy.116
  790.0 12.6 copy.88
  802.6 5.4 copy.117
  815.6 4.6 fusion.85
  820.3 53.9 %reduce-scatter.25.cloned.1.call-done = bf16[384,1536]{1,0:T(8,128)(2,1)} async-done(((bf16[1536,1536]{1,0:T(8,128)(2,1)}), bf16[384,1536]{1,0:T(8,128)(2,1)}) %reduce-scatter.25.cloned.1.call-update) | async-done | bytes 1179664
  874.2 3.7 reshape.274
  882.9 79.2 %reduce-scatter.27.cloned.1.call-done = bf16[384,1536]{1,0:T(8,128)(2,1)} async-done(((bf16[1536,1536]{1,0:T(8,128)(2,1)}), bf16[384,1536]{1,0:T(8,128)(2,1)}) %reduce-scatter.27.cloned.1.call-update) | async-done | bytes 1179664
  962.1 3.7 reshape.276
  971.6 9.0 fusion.88
  980.9 10.3 fusion.96
  996.1 4.3 fusion.91
  1000.5 8.7 add_convert_fusion
  1009.2 3.7 copy.89
  1016.4 3.8 fusion.81
  1020.2 42.8 %all-reduce.18 = (f32[768]{0:T(1024)}, f32[768]{0:T(1024)}, f32[768]{0:T(1024)}, f32[3072]{0:T(1024)}, f32[768]{0:T(1024)}, /*index=5*/f32[768]{0:T(1024)}, f32[768]{0:T(1024)}, f32[768]{0:T(1024)}, f32[768]{0:T(1024)}) all-reduce(f32[768]{0:T(1024)} %reduce_sum.182, ...), channel_id=10, replica_groups=mesh['grp'=8,'seq'=4] {'grp','seq'}, use_global_device_ids=true, to_apply=%region_24.25.clone | all-reduce | flops 9216 | bytes 73728
  1078.8 93.4 %reduce-scatter.19.cloned.1.call-done = f32[24,768]{1,0:T(8,128)} async-done(((f32[768,768]{1,0:T(8,128)}), f32[24,768]{1,0:T(8,128)}) %reduce-scatter.19.cloned.1.call-update) | async-done | bytes 73744 | tf_op jit(solution)/shard_map/reduce_scatter | solution.py:307
  1172.2 103.9 %reduce-scatter.15.cloned.1.call-done = f32[24,768]{1,0:T(8,128)} async-done(((f32[768,768]{1,0:T(8,128)}), f32[24,768]{1,0:T(8,128)}) %reduce-scatter.15.cloned.1.call-update) | async-done | bytes 73744 | tf_op jit(solution)/shard_map/reduce_scatter | solution.py:305
  1276.1 104.6 %reduce-scatter.17.cloned.1.call-done = f32[24,768]{1,0:T(8,128)} async-done(((f32[768,768]{1,0:T(8,128)}), f32[24,768]{1,0:T(8,128)}) %reduce-scatter.17.cloned.1.call-update) | async-done | bytes 73744 | tf_op jit(solution)/shard_map/reduce_scatter | solution.py:306
  1380.8 140.9 %reduce-scatter.21.cloned.1.call-done = f32[24,3072]{1,0:T(8,128)} async-done(((f32[768,3072]{1,0:T(8,128)}), f32[24,3072]{1,0:T(8,128)}) %reduce-scatter.21.cloned.1.call-update) | async-done | bytes 294928 | tf_op jit(solution)/shard_map/reduce_scatter | solution.py:308
  1521.6 142.0 %reduce-scatter.23.cloned.1.call-done = f32[96,768]{1,0:T(8,128)} async-done(((f32[3072,768]{1,0:T(8,128)}), f32[96,768]{1,0:T(8,128)}) %reduce-scatter.23.cloned.1.call-update) | async-done | bytes 294928 | tf_op jit(solution)/shard_map/reduce_scatter | solution.py:309
  (286 shorter events, 169.4 us)
Async XLA Ops:
  7.2 56.4 %copy-start.2 = (bf16[1,2,384,768]{3,2,1,0:T(8,128)(2,1)S(1)}, bf16[1,2,384,768]{3,2,1,0:T(8,128)(2,1)}, u32[]{:S(2)}) copy-start(bf16[1,2,384,768]{3,2,1,0:T(8,128)(2,1)} %param.22) | copy-start | bytes 3538948
  7.2 60.8 %all-gather.9.cloned.1.call-start = ((), (), s32[]{:S(2)}) async-start(), calls=%async_computation.8 | async-start | bytes 1216512 | tf_op jit(solution)/shard_map/all_gather | solution.py:105
  7.9 115.8 %all-gather.15.cloned.1.call-start = ((), (), s32[]{:S(2)}) async-start(), calls=%async_computation.11 | async-start | bytes 1216512 | tf_op jit(solution)/shard_map/all_gather | solution.py:104
  8.7 170.9 %all-gather.13.cloned.1.call-start = ((), (), s32[]{:S(2)}) async-start(), calls=%async_computation.10 | async-start | bytes 1216512 | tf_op jit(solution)/shard_map/all_gather | solution.py:103
  9.4 260.5 %all-gather.11.cloned.1.call-start = ((), (), s32[]{:S(2)}) async-start(), calls=%async_computation.9 | async-start | bytes 5898240 | tf_op jit(solution)/shard_map/all_gather | solution.py:136
  59.7 4.4 copy-start.32
  59.7 4.4 copy-start.21
  61.2 1.8 copy-start.26
  61.2 2.9 copy-start.28
  71.8 288.1 %all-gather.17.cloned.1.call-start = ((), (), s32[]{:S(2)}) async-start(), calls=%async_computation.12 | async-start | bytes 5898240 | tf_op jit(solution)/shard_map/all_gather | solution.py:135
  127.5 294.2 %all-gather.19.cloned.1.call-start = ((), (), s32[]{:S(2)}) async-start(), calls=%async_computation.13 | async-start | bytes 1216512 | tf_op jit(solution)/shard_map/all_gather | solution.py:106
  128.1 352.4 %all-gather.21.cloned.1.call-start = ((), (), s32[]{:S(2)}) async-start(), calls=%async_computation.14 | async-start | bytes 4866048 | tf_op jit(solution)/shard_map/all_gather | solution.py:107
  128.8 416.9 %all-gather.23.cloned.1.call-start = ((), (), s32[]{:S(2)}) async-start(), calls=%async_computation.15 | async-start | bytes 4866048 | tf_op jit(solution)/shard_map/all_gather | solution.py:108
  129.6 744.6 %reduce-scatter.25.cloned.1.call-start = ((), (), s32[]{:S(2)}) async-start(), calls=%async_computation.22 | async-start | bytes 5898240
  359.9 5.1 copy-start.24
  419.2 2.5 copy-start.4
  419.2 2.5 copy-start.35
  425.6 120.1 %copy-start.8 = (bf16[1,2,384,768]{3,2,1,0:T(8,128)(2,1)S(1)}, bf16[1,2,384,768]{3,2,1,0:T(8,128)(2,1)}, u32[]{:S(2)}) copy-start(bf16[1,2,384,768]{3,2,1,0:T(8,128)(2,1)} %param.24) | copy-start | bytes 3538948
  545.7 10.2 copy-start.18
  545.7 10.2 copy-start.37
  555.9 4.9 copy-start.9
  560.8 3.1 copy-start.39
  562.5 1.5 copy-start.6
  571.1 3.3 copy-start.25
  573.7 9.5 copy-start.1
  592.6 9.2 copy-start
  604.8 3.3 copy-start.25
  607.4 9.5 copy-start.1
  626.3 9.2 copy-start
  638.4 3.3 copy-start.25
  641.0 9.5 copy-start.1
  659.9 9.2 copy-start
  672.0 3.3 copy-start.25
  674.6 9.5 copy-start.1
  693.5 9.2 copy-start
  705.7 3.3 copy-start.25
  708.2 9.5 copy-start.1
  727.1 9.2 copy-start
  739.3 3.3 copy-start.25
  741.9 9.5 copy-start.1
  760.8 9.3 copy-start
  789.9 172.2 %reduce-scatter.27.cloned.1.call-start = ((), (), s32[]{:S(2)}) async-start(), calls=%async_computation.23 | async-start | bytes 5898240
  808.0 1.3 copy-start.3
  808.0 1.3 copy-start.22
  808.0 1.3 copy-start.27
  808.0 270.8 %reduce-scatter.13.cloned.1.call-start = ((), (), s32[]{:S(2)}) async-start(), calls=%async_computation.16 | async-start | bytes 2433024 | tf_op jit(solution)/shard_map/reduce_scatter | solution.py:304
  809.2 1.3 copy-start.5
  810.5 1.5 copy-start.15
  815.6 356.6 %reduce-scatter.19.cloned.1.call-start = ((), (), s32[]{:S(2)}) async-start(), calls=%async_computation.19 | async-start | bytes 2433024 | tf_op jit(solution)/shard_map/reduce_scatter | solution.py:307
  820.2 455.9 %reduce-scatter.15.cloned.1.call-start = ((), (), s32[]{:S(2)}) async-start(), calls=%async_computation.17 | async-start | bytes 2433024 | tf_op jit(solution)/shard_map/reduce_scatter | solution.py:305
  877.8 2.5 copy-start.16
  882.9 497.9 %reduce-scatter.17.cloned.1.call-start = ((), (), s32[]{:S(2)}) async-start(), calls=%async_computation.18 | async-start | bytes 2433024 | tf_op jit(solution)/shard_map/reduce_scatter | solution.py:306
  965.8 2.5 copy-start.17
  970.9 550.7 %reduce-scatter.21.cloned.1.call-start = ((), (), s32[]{:S(2)}) async-start(), calls=%async_computation.20 | async-start | bytes 9732096 | tf_op jit(solution)/shard_map/reduce_scatter | solution.py:308
  980.6 683.1 %reduce-scatter.23.cloned.1.call-start = ((), (), s32[]{:S(2)}) async-start(), calls=%async_computation.21 | async-start | bytes 9732096 | tf_op jit(solution)/shard_map/reduce_scatter | solution.py:309
  1009.2 4.5 copy-start.12
  1013.7 2.6 copy-start.14
  1013.7 2.6 copy-start.23
  1013.7 2.6 copy-start.29
  1013.7 2.6 copy-start.31
  1013.7 2.6 copy-start.38
  1013.7 2.7 copy-start.40
  1016.4 3.8 copy-start.34
  1016.4 59.3 %copy-start.7 = (f32[768,768]{1,0:T(8,128)S(1)}, f32[768,768]{1,0:T(8,128)}, u32[]{:S(2)}) copy-start(f32[768,768]{1,0:T(8,128)} %copy-done.6) | copy-start | bytes 7077892
  (8 other events, 6.8 us)
Sparse Core Ops, SparseCore 0:
  10.8 57.1 all-gather.8
  70.8 52.8 all-gather.14
  126.5 53.0 all-gather.12
  181.6 88.2 all-gather.10
  272.0 87.8 all-gather.16
  362.5 52.6 all-gather.18
  418.0 62.4 all-gather.20
  483.3 62.3 all-gather.22
  790.0 84.0 reduce-scatter.24
  876.3 85.7 reduce-scatter.26
  968.0 99.5 reduce-scatter.12
  1074.1 98.0 reduce-scatter.18
  1178.1 98.0 reduce-scatter.14
  1282.7 98.0 reduce-scatter.16
  1387.1 134.5 reduce-scatter.20
  1529.0 134.6 reduce-scatter.22
where the time goes:
time: 1680 us; the launch traced here: 1670 us
  waiting for transfers between devices  1090 us (65%)
  matrix products  278 us (17%)
  local copies, waits for them, and re-layouts  110 us (7%)
  other arithmetic  95 us (6%)
  blocking collectives  85.5 us (5%)
    reduce_scatter x1, waiting for transfers between devices, body(): lax.psum_scatter(grad_down, ('grp', 'seq'), scatter_dimension=0, tiled=True)  142 us
    reduce_scatter x1, waiting for transfers between devices, body(): lax.psum_scatter(grad_up, ('grp', 'seq'), scatter_dimension=0, tiled=True)  141 us
    unnamed x18, waiting for transfers between devices  137 us
    reduce_scatter x1, waiting for transfers between devices, body(): lax.psum_scatter(gw_value, ('grp', 'seq'), scatter_dimension=0, tiled=True)  105 us
    reduce_scatter x1, waiting for transfers between devices, body(): lax.psum_scatter(gw_key, ('grp', 'seq'), scatter_dimension=0, tiled=True)  104 us
    reduce_scatter x1, waiting for transfers between devices, body(): lax.psum_scatter(grad_out, ('grp', 'seq'), scatter_dimension=0, tiled=True)  93.4 us
    all_gather x1, waiting for transfers between devices, body(): lax.all_gather(value_local.reshape(slot_count, slice_len, width), 'seq',...  86.8 us
    unnamed x2, blocking collectives  85.5 us
  transfers between devices with their start and end apart: 16, of which 14 were waited for; matrix products, arithmetic and copies ran while one was open for 14% of the time, Pallas kernels for 0%

commit v1 on v0

--- a/solution.py
+++ b/solution.py
@@ -8,6 +8,28 @@
 score_scale = 0.125
 sqrt_half = 0.7071067811865476
 inv_root_tau = 0.3989422804014327
+
+
+def joined_along(blocks, dim):
+    shape = list(blocks.shape[1:])
+    shape[dim] *= blocks.shape[0]
+    return jnp.moveaxis(blocks, 0, dim).reshape(shape)
+
+
+def collect(x, axis, dim):
+    length = lax.axis_size(axis)
+    pairs = [(i, (i + 1) % length) for i in range(length)]
+    back = [(b, a) for a, b in pairs]
+    lower, upper = ([], [])
+    for hop in range(length - 1):
+        if hop % 2 == 0:
+            lower.append(lax.ppermute(lower[-1] if lower else x, axis, pairs))
+        else:
+            upper.append(lax.ppermute(upper[-1] if upper else x, axis, back))
+    pieces = jnp.stack([*lower[::-1], x, *upper])
+    shift = lax.axis_index(axis) - len(lower)
+    pieces = pieces[(jnp.arange(length) - shift) % length]
+    return joined_along(pieces, dim)
 
 
 def standardize(token_rows):
@@ -133,9 +155,7 @@
     ).astype(jnp.bfloat16)
     key_all, value_all = (
         lax.all_gather(key_local.reshape(slot_count, slice_len, width), "seq", axis=1, tiled=True),
-        lax.all_gather(
-            value_local.reshape(slot_count, slice_len, width), "seq", axis=1, tiled=True
-        ),
+        collect(value_local.reshape(slot_count, slice_len, width), "seq", 1),
     )
     clip_len = key_all.shape[1]
     offsets = jnp.arange(clip_len, dtype=jnp.int32) % slice_len

time: 1680 us -> 1620 us (0.964)
  waiting for transfers between devices: 1090 us -> 1000 us
  local copies, waits for them, and re-layouts: 110 us -> 132 us
    all_gather x1 -> x0, waiting for transfers between devices: 86.8 us -> none  [body(): lax.all_gather(value_local.reshape(slot_count, slice_len, width), 'seq',...]
    all_gather x1, waiting for transfers between devices: 51.8 us -> 3.83 us  [body(): lax.all_gather(shards[1], ('grp', 'seq'), axis=0, tiled=True)]
    all_gather x1, waiting for transfers between devices: 3.89 us -> 50 us  [body(): lax.all_gather(shards[2], ('grp', 'seq'), axis=0, tiled=True)]
    all_gather x1, waiting for transfers between devices: 84.9 us -> 52.5 us  [body(): lax.all_gather(key_local.reshape(slot_count, slice_len, width), 'seq', ax...]
    ppermute x0 -> x3, waiting for transfers between devices: none -> 27.9 us  [the longest x2 27.9 us: collect(): lower.append(lax.ppermute(lower[-1] if lower else x, axis, pairs))]
    unnamed x18 -> x17, waiting for transfers between devices: 137 us -> 136 us
    unnamed x115 -> x119, local copies, waits for them, and re-layouts: 85.1 us -> 85.2 us
  transfers between devices with their start and end apart: 16 -> 18, of which waited for: 14 -> 14; matrix products, arithmetic and copies ran while one was open for 14% -> 16% of each run, Pallas kernels for 0% -> 0%
where the time goes in v1:
time: 1620 us; the launch traced here: 1610 us
  waiting for transfers between devices  1000 us (62%)
  matrix products  279 us (17%)
  local copies, waits for them, and re-layouts  132 us (8%)
  other arithmetic  97.2 us (6%)
  blocking collectives  85.6 us (5%)
    reduce_scatter x1, waiting for transfers between devices, body(): lax.psum_scatter(grad_down, ('grp', 'seq'), scatter_dimension=0, tiled=True)  142 us
    reduce_scatter x1, waiting for transfers between devices, body(): lax.psum_scatter(grad_up, ('grp', 'seq'), scatter_dimension=0, tiled=True)  141 us
    unnamed x17, waiting for transfers between devices  136 us
    reduce_scatter x1, waiting for transfers between devices, body(): lax.psum_scatter(gw_value, ('grp', 'seq'), scatter_dimension=0, tiled=True)  105 us
    reduce_scatter x1, waiting for transfers between devices, body(): lax.psum_scatter(gw_key, ('grp', 'seq'), scatter_dimension=0, tiled=True)  104 us
    reduce_scatter x1, waiting for transfers between devices, body(): lax.psum_scatter(grad_out, ('grp', 'seq'), scatter_dimension=0, tiled=True)  93.5 us
    unnamed x2, blocking collectives  85.6 us
    unnamed x119, local copies, waits for them, and re-layouts  85.2 us
  transfers between devices with their start and end apart: 18, of which 14 were waited for; matrix products, arithmetic and copies ran while one was open for 16% of the time, Pallas kernels for 0%

profile of v1, /device:TPU:0, one launch (start us, length us, event | category | flops | bytes accessed | tf_op | source)
XLA Modules:
  0.0 1614.7 jit_solution(13753669330162857276)
XLA Ops:
  17.0 42.7 %all-reduce.19 = (bf16[768]{0:T(1024)(128)(2,1)S(1)}, bf16[768]{0:T(1024)(128)(2,1)S(1)}, bf16[768]{0:T(1024)(128)(2,1)}, bf16[768]{0:T(1024)(128)(2,1)}, bf16[7...) all-reduce(bf16[768]{0:T(1024)(128)(2,1)S(1)} %dynamic-update-slice, ...), channel_id=1, replica_groups=mesh['grp'=8,'seq'=4] {'grp','seq'}, use_global_device_ids=true, to_apply=%add.1 | all-reduce | flops 9216 | bytes 36864
  64.2 3.8 all-gather.12.cloned.1.call-done
  73.7 50.0 %all-gather.8.cloned.1.call-done = bf16[768,768]{1,0:T(8,128)(2,1)} async-done(((bf16[24,768]{1,0:T(8,128)(2,1)}), bf16[768,768]{1,0:T(8,128)(2,1)}) %all-gather.8.cloned.1.call-update) | async-done | bytes 1179664 | tf_op jit(solution)/shard_map/all_gather | solution.py:127
  130.9 27.9 %collective-permute-done = bf16[2,384,768]{2,1,0:T(8,128)(2,1)} collective-permute-done((bf16[2,384,768]{2,1,0:T(8,128)(2,1)}, bf16[2,384,768]{2,1,0:T(8,128)(2,1)}, u32[]{:S(2)}, u32[]{:S(2)}) %collective-permute-start) | collective-permute-done | bytes 1179680 | tf_op jit(solution)/shard_map/ppermute | solution.py:26
  161.4 53.9 %all-gather.10.cloned.1.call-done = bf16[768,768]{1,0:T(8,128)(2,1)} async-done(((bf16[24,768]{1,0:T(8,128)(2,1)}), bf16[768,768]{1,0:T(8,128)(2,1)}) %all-gather.10.cloned.1.call-update) | async-done | bytes 1179664 | tf_op jit(solution)/shard_map/all_gather | solution.py:125
  219.1 4.2 pad_maximum_fusion
  223.3 5.7 gather_fusion
  229.0 8.6 copy.68
  237.6 8.8 reshape_reshape.11
  246.4 5.0 copy.71
  251.4 52.5 %all-gather.14.cloned.1.call-done = bf16[2,1536,768]{1,2,0:T(8,128)(2,1)} async-done(((bf16[2,384,768]{1,2,0:T(8,128)(2,1)}), bf16[2,1536,768]{1,2,0:T(8,128)(2,1)}) %all-gather.14.cloned.1.call-update) | async-done | bytes 4718608 | tf_op jit(solution)/shard_map/all_gather | solution.py:157
  304.0 5.0 copy.73
  309.1 54.2 %while.28 = (s32[]{:T(128)}, bf16[6,2,384,2,64]{2,4,3,1,0:T(8,128)(2,1)S(1)}, f32[6,2,2,384]{3,2,1,0:T(2,128)}, bf16[6,2,1536,2,64]{2,4,3,1,0:T(8,128)(2,1)}, bf...) while((s32[]{:T(128)}, ...), condition=%wide.region_5.6_spmd.clone, body=%wide.region_2.5_spmd.clone.sunk | while | flops 632292864 | bytes 30550128 | solution.py:188
  369.7 54.7 %all-gather.18.cloned.1.call-done = bf16[768,3072]{1,0:T(8,128)(2,1)} async-done(((bf16[24,3072]{1,0:T(8,128)(2,1)}), bf16[768,3072]{1,0:T(8,128)(2,1)}) %all-gather.18.cloned.1.call-update) | async-done | bytes 4718608 | tf_op jit(solution)/shard_map/all_gather | solution.py:129
  424.4 28.1 %fusion.49 = (bf16[768,3072]{1,0:T(8,128)(2,1)}, f32[768,3072]{1,0:T(8,128)}) fusion(f32[3072]{0:T(1024)} %convert_element_type.182, bf16[768,3072]{1,0:T(8,128)(2,1)} %all-gather.18.cloned.1.call-done, f32[768,768]{1,0:T(8,128)S(1)} %get-tuple-element.288, f32[768]{0:T(1024)} %convert_element_type.180, f32[768]{0:T(1024)S(1)} %convert_element_type.179, ...), kind=kOutput, calls=%fused_computation.60 | convolution fusion | flops 3782541312 | bytes 21258240 | tf_op jit(solution)/shard_map/dot_general | solution.py:198
  452.5 37.1 %all-gather.20.cloned.1.call-done = bf16[3072,768]{1,0:T(8,128)(2,1)} async-done(((bf16[96,768]{1,0:T(8,128)(2,1)}), bf16[3072,768]{1,0:T(8,128)(2,1)}) %all-gather.20.cloned.1.call-update) | async-done | bytes 4718608 | tf_op jit(solution)/shard_map/all_gather | solution.py:130
  489.6 10.2 convert_reduce_fusion
  499.8 4.9 multiply_reduce_fusion.1
  514.0 201.9 %while.29 = (s32[]{:T(128)}, bf16[6,2,384,2,64]{2,4,3,1,0:T(8,128)(2,1)}, bf16[6,2,1536,2,64]{2,4,3,0,1:T(8,128)(2,1)}, bf16[6,2,1536,2,64]{2,4,3,0,1:T(8,128)(2...) while((s32[]{:T(128)}, ...), condition=%wide.region_12.13_spmd.clone, body=%wide.region_10.12_spmd.clone.sunk | while | flops 1531676160 | bytes 153400592 | solution.py:297
  518.4 8.7 multiply_reduce_fusion.7
  527.1 9.4 multiply_convert_fusion.2
  536.5 4.9 fusion.158
  541.5 4.3 fusion.159
  552.1 8.7 multiply_reduce_fusion.7
  560.8 9.4 multiply_convert_fusion.2
  570.2 4.9 fusion.158
  575.1 4.3 fusion.159
  585.8 8.7 multiply_reduce_fusion.7
  594.5 9.4 multiply_convert_fusion.2
  603.9 4.9 fusion.158
  608.8 4.3 fusion.159
  619.4 8.7 multiply_reduce_fusion.7
  628.1 9.4 multiply_convert_fusion.2
  637.5 4.9 fusion.158
  642.4 4.3 fusion.159
  653.1 8.7 multiply_reduce_fusion.7
  661.8 9.4 multiply_convert_fusion.2
  671.2 4.9 fusion.158
  676.1 4.3 fusion.159
  686.7 8.7 multiply_reduce_fusion.7
  695.4 9.4 multiply_convert_fusion.2
  704.8 4.9 fusion.158
  709.7 4.3 fusion.159
  715.9 12.5 copy.85
  728.4 5.5 copy.115
  734.0 12.6 copy.87
  746.6 5.4 copy.116
  759.6 4.6 fusion.87
  764.3 53.9 %reduce-scatter.25.cloned.1.call-done = bf16[384,1536]{1,0:T(8,128)(2,1)} async-done(((bf16[1536,1536]{1,0:T(8,128)(2,1)}), bf16[384,1536]{1,0:T(8,128)(2,1)}) %reduce-scatter.25.cloned.1.call-update) | async-done | bytes 1179664
  818.1 3.7 reshape.327
  826.9 79.3 %reduce-scatter.27.cloned.1.call-done = bf16[384,1536]{1,0:T(8,128)(2,1)} async-done(((bf16[1536,1536]{1,0:T(8,128)(2,1)}), bf16[384,1536]{1,0:T(8,128)(2,1)}) %reduce-scatter.27.cloned.1.call-update) | async-done | bytes 1179664
  906.3 3.7 reshape.329
  915.7 9.0 fusion.90
  925.0 10.3 fusion.98
  940.3 4.3 fusion.93
  944.6 8.7 add_convert_fusion
  953.3 3.7 copy.88
  960.5 3.8 fusion.81
  964.3 43.0 %all-reduce.18 = (f32[768]{0:T(1024)}, f32[768]{0:T(1024)}, f32[768]{0:T(1024)}, f32[3072]{0:T(1024)}, f32[768]{0:T(1024)}, /*index=5*/f32[768]{0:T(1024)}, f32[768]{0:T(1024)}, f32[768]{0:T(1024)}, f32[768]{0:T(1024)}) all-reduce(f32[768]{0:T(1024)} %reduce_sum.182, ...), channel_id=10, replica_groups=mesh['grp'=8,'seq'=4] {'grp','seq'}, use_global_device_ids=true, to_apply=%region_24.25.clone | all-reduce | flops 9216 | bytes 73728
  1023.0 93.5 %reduce-scatter.19.cloned.1.call-done = f32[24,768]{1,0:T(8,128)} async-done(((f32[768,768]{1,0:T(8,128)}), f32[24,768]{1,0:T(8,128)}) %reduce-scatter.19.cloned.1.call-update) | async-done | bytes 73744 | tf_op jit(solution)/shard_map/reduce_scatter | solution.py:327
  1116.5 103.8 %reduce-scatter.15.cloned.1.call-done = f32[24,768]{1,0:T(8,128)} async-done(((f32[768,768]{1,0:T(8,128)}), f32[24,768]{1,0:T(8,128)}) %reduce-scatter.15.cloned.1.call-update) | async-done | bytes 73744 | tf_op jit(solution)/shard_map/reduce_scatter | solution.py:325
  1220.2 104.8 %reduce-scatter.17.cloned.1.call-done = f32[24,768]{1,0:T(8,128)} async-done(((f32[768,768]{1,0:T(8,128)}), f32[24,768]{1,0:T(8,128)}) %reduce-scatter.17.cloned.1.call-update) | async-done | bytes 73744 | tf_op jit(solution)/shard_map/reduce_scatter | solution.py:326
  1325.0 140.7 %reduce-scatter.21.cloned.1.call-done = f32[24,3072]{1,0:T(8,128)} async-done(((f32[768,3072]{1,0:T(8,128)}), f32[24,3072]{1,0:T(8,128)}) %reduce-scatter.21.cloned.1.call-update) | async-done | bytes 294928 | tf_op jit(solution)/shard_map/reduce_scatter | solution.py:328
  1465.7 142.0 %reduce-scatter.23.cloned.1.call-done = f32[96,768]{1,0:T(8,128)} async-done(((f32[3072,768]{1,0:T(8,128)}), f32[96,768]{1,0:T(8,128)}) %reduce-scatter.23.cloned.1.call-update) | async-done | bytes 294928 | tf_op jit(solution)/shard_map/reduce_scatter | solution.py:329
  (298 shorter events, 184.1 us)
Async XLA Ops:
  7.2 56.4 %copy-start.2 = (bf16[1,2,384,768]{3,2,1,0:T(8,128)(2,1)S(1)}, bf16[1,2,384,768]{3,2,1,0:T(8,128)(2,1)}, u32[]{:S(2)}) copy-start(bf16[1,2,384,768]{3,2,1,0:T(8,128)(2,1)} %param.22) | copy-start | bytes 3538948
  7.2 60.8 %all-gather.12.cloned.1.call-start = ((), (), s32[]{:S(2)}) async-start(), calls=%async_computation.10 | async-start | bytes 1216512 | tf_op jit(solution)/shard_map/all_gather | solution.py:126
  7.9 115.8 %all-gather.8.cloned.1.call-start = ((), (), s32[]{:S(2)}) async-start(), calls=%async_computation.8 | async-start | bytes 1216512 | tf_op jit(solution)/shard_map/all_gather | solution.py:127
  8.7 206.6 %all-gather.10.cloned.1.call-start = ((), (), s32[]{:S(2)}) async-start(), calls=%async_computation.9 | async-start | bytes 1216512 | tf_op jit(solution)/shard_map/all_gather | solution.py:125
  9.4 294.5 %all-gather.14.cloned.1.call-start = ((), (), s32[]{:S(2)}) async-start(), calls=%async_computation.11 | async-start | bytes 5898240 | tf_op jit(solution)/shard_map/all_gather | solution.py:157
  59.7 4.4 copy-start.32
  59.7 4.4 copy-start.21
  61.2 1.8 copy-start.26
  61.2 2.9 copy-start.28
  71.8 294.0 %all-gather.16.cloned.1.call-start = ((), (), s32[]{:S(2)}) async-start(), calls=%async_computation.12 | async-start | bytes 1216512 | tf_op jit(solution)/shard_map/all_gather | solution.py:128
  72.4 352.0 %all-gather.18.cloned.1.call-start = ((), (), s32[]{:S(2)}) async-start(), calls=%async_computation.13 | async-start | bytes 4866048 | tf_op jit(solution)/shard_map/all_gather | solution.py:129
  73.0 416.6 %all-gather.20.cloned.1.call-start = ((), (), s32[]{:S(2)}) async-start(), calls=%async_computation.14 | async-start | bytes 4866048 | tf_op jit(solution)/shard_map/all_gather | solution.py:130
  73.7 85.2 %copy-start.38 = (bf16[768]{0:T(1024)(128)(2,1)S(1)}, bf16[768]{0:T(1024)(128)(2,1)}, u32[]{:S(2)}) copy-start(bf16[768]{0:T(1024)(128)(2,1)} %get-tuple-element.276) | copy-start | bytes 4612
  73.7 85.8 %copy-start.37 = (bf16[768]{0:T(1024)(128)(2,1)S(1)}, bf16[768]{0:T(1024)(128)(2,1)}, u32[]{:S(2)}) copy-start(bf16[768]{0:T(1024)(128)(2,1)} %get-tuple-element.275) | copy-start | bytes 4612
  127.1 31.8 %collective-permute-start = (bf16[2,384,768]{2,1,0:T(8,128)(2,1)}, bf16[2,384,768]{2,1,0:T(8,128)(2,1)}, u32[]{:S(2)}, u32[]{:S(2)}) collective-permute-start(bf16[2,384,768]{2,1,0:T(8,128)(2,1)} %bitcast.1), channel_id=1, source_target_pairs={{0,1},{1,2},{2,3},{3,0},{4,5},{5,6},{6,7},{7,4},{8,9},{9,10},{10,1... | collective-permute-start | bytes 3538952 | tf_op jit(solution)/shard_map/ppermute | solution.py:26
  127.6 91.4 %collective-permute-start.2 = (bf16[2,384,768]{2,1,0:T(8,128)(2,1)}, bf16[2,384,768]{2,1,0:T(8,128)(2,1)}, u32[]{:S(2)}, u32[]{:S(2)}) collective-permute-start(bf16[2,384,768]{2,1,0:T(8,128)(2,1)} %bitcast.1), channel_id=1, source_target_pairs={{1,0},{2,1},{3,2},{0,3},{5,4},{6,5},{7,6},{4,7},{9,8},{10,9},{11,1... | collective-permute-start | bytes 3538952 | tf_op jit(solution)/shard_map/ppermute | solution.py:28
  158.8 60.2 %collective-permute-start.1 = (bf16[2,384,768]{2,1,0:T(8,128)(2,1)}, bf16[2,384,768]{2,1,0:T(8,128)(2,1)}, u32[]{:S(2)}, u32[]{:S(2)}) collective-permute-start(bf16[2,384,768]{2,1,0:T(8,128)(2,1)} %collective-permute-done), channel_id=1, source_target_pairs={{0,1},{1,2},{2,3},{3,0},{4,5},{5,6},{6,7},{7,4},{8,9},{9,10},{10,1... | collective-permute-start | bytes 3538952 | tf_op jit(solution)/shard_map/ppermute | solution.py:26
  158.9 659.3 %reduce-scatter.25.cloned.1.call-start = ((), (), s32[]{:S(2)}) async-start(), calls=%async_computation.21 | async-start | bytes 5898240
  304.0 5.1 copy-start.24
  363.3 2.5 copy-start.4
  363.3 2.5 copy-start.35
  369.7 119.9 %copy-start.8 = (bf16[1,2,384,768]{3,2,1,0:T(8,128)(2,1)S(1)}, bf16[1,2,384,768]{3,2,1,0:T(8,128)(2,1)}, u32[]{:S(2)}) copy-start(bf16[1,2,384,768]{3,2,1,0:T(8,128)(2,1)} %param.24) | copy-start | bytes 3538948
  489.6 10.2 copy-start.18
  489.6 10.2 copy-start.39
  499.8 4.9 copy-start.9
  504.7 3.1 copy-start.41
  506.4 1.5 copy-start.6
  515.0 3.3 copy-start.25
  517.6 9.5 copy-start.1
  536.5 9.2 copy-start
  548.7 3.3 copy-start.25
  551.3 9.5 copy-start.1
  570.2 9.3 copy-start
  582.4 3.3 copy-start.25
  584.9 9.5 copy-start.1
  603.9 9.2 copy-start
  616.0 3.3 copy-start.25
  618.6 9.5 copy-start.1
  637.5 9.3 copy-start
  649.7 3.3 copy-start.25
  652.2 9.5 copy-start.1
  671.2 9.2 copy-start
  683.3 3.3 copy-start.25
  685.9 9.5 copy-start.1
  704.8 9.3 copy-start
  733.9 172.3 %reduce-scatter.27.cloned.1.call-start = ((), (), s32[]{:S(2)}) async-start(), calls=%async_computation.22 | async-start | bytes 5898240
  752.0 271.0 %reduce-scatter.13.cloned.1.call-start = ((), (), s32[]{:S(2)}) async-start(), calls=%async_computation.15 | async-start | bytes 2433024 | tf_op jit(solution)/shard_map/reduce_scatter | solution.py:324
  754.5 1.5 copy-start.15
  759.6 356.9 %reduce-scatter.19.cloned.1.call-start = ((), (), s32[]{:S(2)}) async-start(), calls=%async_computation.18 | async-start | bytes 2433024 | tf_op jit(solution)/shard_map/reduce_scatter | solution.py:327
  764.2 456.0 %reduce-scatter.15.cloned.1.call-start = ((), (), s32[]{:S(2)}) async-start(), calls=%async_computation.16 | async-start | bytes 2433024 | tf_op jit(solution)/shard_map/reduce_scatter | solution.py:325
  821.8 2.5 copy-start.16
  826.9 498.1 %reduce-scatter.17.cloned.1.call-start = ((), (), s32[]{:S(2)}) async-start(), calls=%async_computation.17 | async-start | bytes 2433024 | tf_op jit(solution)/shard_map/reduce_scatter | solution.py:326
  909.9 2.5 copy-start.17
  915.0 550.6 %reduce-scatter.21.cloned.1.call-start = ((), (), s32[]{:S(2)}) async-start(), calls=%async_computation.19 | async-start | bytes 9732096 | tf_op jit(solution)/shard_map/reduce_scatter | solution.py:328
  924.7 683.0 %reduce-scatter.23.cloned.1.call-start = ((), (), s32[]{:S(2)}) async-start(), calls=%async_computation.20 | async-start | bytes 9732096 | tf_op jit(solution)/shard_map/reduce_scatter | solution.py:329
  953.3 4.5 copy-start.12
  957.8 2.6 copy-start.14
  957.8 2.6 copy-start.23
  957.8 2.6 copy-start.29
  957.8 2.6 copy-start.31
  957.8 2.6 copy-start.40
  957.8 2.7 copy-start.42
  960.5 3.8 copy-start.34
  960.5 59.4 %copy-start.7 = (f32[768,768]{1,0:T(8,128)S(1)}, f32[768,768]{1,0:T(8,128)}, u32[]{:S(2)}) copy-start(f32[768,768]{1,0:T(8,128)} %copy-done.6) | copy-start | bytes 7077892
  (12 other events, 11.4 us)
Sparse Core Ops, SparseCore 0:
  10.8 57.1 all-gather.11
  70.8 52.8 all-gather.7
  126.5 88.7 all-gather.9
  217.3 86.5 all-gather.13
  306.6 52.6 all-gather.15
  361.9 62.4 all-gather.17
  427.2 62.3 all-gather.19
  734.0 84.0 reduce-scatter.24
  820.4 85.7 reduce-scatter.26
  912.0 99.6 reduce-scatter.12
  1018.4 98.0 reduce-scatter.18
  1122.2 97.9 reduce-scatter.14
  1226.9 98.0 reduce-scatter.16
  1331.3 134.3 reduce-scatter.20
  1473.0 134.6 reduce-scatter.22
